TPU v7x, 32 devices: a whole 2x2x4 slice. The times are simulated.
32 devices in a mesh: req: 4 (over y, core), exp: 8 (over z, x).
Axes of the slice: x: 2, y: 2, z: 4, core: 2. Of those that a mesh axis runs over, the one named last changes fastest.
Arguments:
- queries: bfloat16 [8, 512, 2048], P('req', None, 'exp'), may hold values from -40 to 40
- new_entries: bfloat16 [8, 2, 512, 2048], P('req', None, None, 'exp'), may hold values from -40 to 40
- cache_entries: bfloat16 [8, 2, 4096, 2048], P('req', None, None, 'exp'), may hold values from -6 to 6
- cache_lengths: int32 [8], P('req'), may hold values from 1 to 4096, 16384 in all
- out_proj: bfloat16 [2048, 2048], P('exp'), may hold values from -0.125 to 0.125
- residual: bfloat16 [4096, 2048], P(('req', 'exp')), may hold values from -40 to 40
- norm_gain: float32 [2048], replicated, may hold values from 0.1 to 1.9
- routes: int32 [4096, 8], P(('req', 'exp')), may hold values from 0 to 63, all different within a row; in each aligned block of 128 rows (0 to 127, 128 to 255, ...) at most 20 rows name the same one
- gate_weights: float32 [4096, 8], P(('req', 'exp')), may hold values from 0.1 to 0.6
- expert_in: bfloat16 [2, 2048, 65536], P(None, None, ('req', 'exp')), may hold values from -0.125 to 0.125
- expert_down: bfloat16 [65536, 2048], P(('req', 'exp')), may hold values from -0.1875 to 0.1875
Outputs:
- attended: bfloat16 [4096, 2048], P(('req', 'exp'))
- expert_out: bfloat16 [4096, 2048], P(('req', 'exp'))
Inputs may be any that keep to these rules, and one draw needn't show every extreme that they name: `cache_lengths`: the lengths add up to 16384 and one is exactly 4096. `routes`: each row names 8 different experts; within the rows of one device (aligned blocks of 128 rows) no expert is named more than 20 times, a bound that some block reaches.
All inputs are finite; a program needn't handle non-finite values. No bound on the sum of `cache_lengths` on one device may be relied on, other than what follows from the above.
Results may differ from a plain program's by a relative error of at most 0.0085.
Values may be sent and summed in bfloat16 or wider, within the bound.
A program may use at most 128 MiB of HBM per device.

v0:
```python
import jax
import jax.numpy as jnp
from jax import lax
from jax.sharding import PartitionSpec as P

HD = 128
EXPERTS = 64
FF = 1024
TOP = 8


def local(
    queries,
    new_entries,
    cache_entries,
    cache_lengths,
    out_proj,
    residual,
    norm_gain,
    routes,
    gate_weights,
    expert_in,
    expert_down,
):
    req_local, new_len, width_local = queries.shape
    heads_local = width_local // HD
    cache_len = cache_entries.shape[2]
    tok_local = residual.shape[0]
    model_width = residual.shape[1]

    def attend_request(packed):
        query_rows, new_rows, cache_rows, length = packed
        query_heads = query_rows.reshape(new_len, heads_local, HD)
        cache_keys = cache_rows[0].reshape(cache_len, heads_local, HD)
        cache_vals = cache_rows[1].reshape(cache_len, heads_local, HD)
        new_keys = new_rows[0].reshape(new_len, heads_local, HD)
        new_vals = new_rows[1].reshape(new_len, heads_local, HD)
        scale = HD ** (-0.5)
        cache_scores = (
            jnp.einsum("thd,jhd->htj", query_heads, cache_keys, preferred_element_type=jnp.float32)
            * scale
        )
        new_scores = (
            jnp.einsum("thd,jhd->htj", query_heads, new_keys, preferred_element_type=jnp.float32)
            * scale
        )
        cache_valid = jnp.arange(cache_len, dtype=jnp.int32) < length
        causal = (
            jnp.arange(new_len, dtype=jnp.int32)[None, :]
            <= jnp.arange(new_len, dtype=jnp.int32)[:, None]
        )
        scores = jnp.concatenate(
            [
                jnp.where(cache_valid[None, None, :], cache_scores, -1e30),
                jnp.where(causal[None, :, :], new_scores, -1e30),
            ],
            axis=-1,
        )
        peak = jnp.max(scores, axis=-1, keepdims=True)
        weights = jnp.exp(scores - peak)
        denoms = jnp.sum(weights, axis=-1)
        weights_bf = weights.astype(jnp.bfloat16)
        all_vals = jnp.concatenate([cache_vals, new_vals], axis=0)
        mixed = jnp.einsum("htj,jhd->thd", weights_bf, all_vals, preferred_element_type=jnp.float32)
        mixed = mixed / jnp.transpose(denoms)[:, :, None]
        return mixed.astype(jnp.bfloat16).reshape(new_len, width_local)

    attention = lax.map(attend_request, (queries, new_entries, cache_entries, cache_lengths))
    attention = attention.reshape(req_local * new_len, width_local)
    projected = lax.psum_scatter(
        jnp.dot(attention, out_proj, preferred_element_type=jnp.float32),
        "exp",
        scatter_dimension=0,
        tiled=True,
    )
    hidden = residual.astype(jnp.float32) + projected
    attended = hidden.astype(jnp.bfloat16)
    mean_square = jnp.mean(hidden * hidden, axis=-1, keepdims=True)
    normed = (hidden * lax.rsqrt(mean_square + 1e-05) * norm_gain).astype(jnp.bfloat16)
    req_count = lax.axis_size("req")
    exp_count = lax.axis_size("exp")
    devices = req_count * exp_count
    half_units = FF // 2
    pieces = expert_in.shape[2] // half_units
    capacity = max(2, tok_local * TOP * 5 // (EXPERTS * 4))
    flat_routes = routes.reshape(-1)
    onehot = (flat_routes[:, None] == jnp.arange(EXPERTS, dtype=jnp.int32)[None, :]).astype(
        jnp.int32
    )
    slot_index = jnp.sum(jnp.cumsum(onehot, axis=0) * onehot, axis=1) - 1
    positions = flat_routes * capacity + slot_index
    slot_rows = (
        jnp.zeros((EXPERTS * capacity, model_width), jnp.bfloat16)
        .at[positions]
        .set(jnp.repeat(normed, TOP, axis=0))
    )
    outgoing = jnp.repeat(slot_rows.reshape(EXPERTS, capacity, model_width), 2, axis=0)
    outgoing = outgoing.reshape(devices, pieces, capacity, model_width)
    arrived = lax.all_to_all(outgoing, ("req", "exp"), split_axis=0, concat_axis=0, tiled=True)
    sources = arrived.shape[0]
    items = arrived.shape[2]
    outputs = []
    for piece_index in range(pieces):
        lower = piece_index * half_units
        rows = arrived[:, piece_index].reshape(sources * items, model_width)
        gate_part = jnp.dot(
            rows, expert_in[0, :, lower : lower + half_units], preferred_element_type=jnp.float32
        )
        up_part = jnp.dot(
            rows, expert_in[1, :, lower : lower + half_units], preferred_element_type=jnp.float32
        )
        inner = (jax.nn.silu(gate_part) * up_part).astype(jnp.bfloat16)
        half_out = jnp.dot(
            inner, expert_down[lower : lower + half_units], preferred_element_type=jnp.float32
        ).astype(jnp.bfloat16)
        outputs.append(half_out.reshape(sources, items, model_width))
    returned = lax.all_to_all(
        jnp.stack(outputs, axis=1), ("req", "exp"), split_axis=0, concat_axis=0, tiled=True
    )
    halves = returned.reshape(EXPERTS, 2, capacity, model_width)
    summed = (halves[:, 0].astype(jnp.float32) + halves[:, 1].astype(jnp.float32)).reshape(
        EXPERTS * capacity, model_width
    )
    picked = summed[positions] * gate_weights.reshape(-1)[:, None]
    expert_out = jnp.sum(picked.reshape(tok_local, TOP, model_width), axis=1).astype(jnp.bfloat16)
    return (attended, expert_out)


def solution(mesh):
    return jax.shard_map(
        local,
        mesh=mesh,
        in_specs=(
            P("req", None, "exp"),
            P("req", None, None, "exp"),
            P("req", None, None, "exp"),
            P("req"),
            P("exp", None),
            P(("req", "exp"), None),
            P(),
            P(("req", "exp"), None),
            P(("req", "exp"), None),
            P(None, None, ("req", "exp")),
            P(("req", "exp"), None),
        ),
        out_specs=(P(("req", "exp"), None), P(("req", "exp"), None)),
        check_vma=False,
    )
```

profile of v0, /device:TPU:0, one launch (start us, length us, event | category | flops | bytes accessed | tf_op | source)
XLA Modules:
  0.0 1098.8 jit_solution(423680183574021900)
XLA Ops:
  7.2 95.3 %while.10 = (s32[]{:T(128)}, bf16[2,512,256]{2,1,0:T(8,128)(2,1)}, bf16[2,2,4096,256]{3,2,1,0:T(8,128)(2,1)}, bf16[2,2,512,256]{3,2,1,0:T(8,128)(2,1)}, s32[2]{0...) while((s32[]{:T(128)}, bf16[2,512,256]{2,1,0:T(8,128)(2,1)}, ...), condition=%wide.region_4.5_spmd, body=%wide.region_0.4_spmd.sunk | while | flops 2463631360 | bytes 83669200 | solution.py:68
  22.6 9.0 fusion.137
  44.3 8.9 fusion.139
  70.2 9.0 fusion.137
  91.9 8.9 fusion.139
  109.3 18.0 %reduce-window.6 = s32[64,8,128]{2,1,0:T(8,128)S(1)} reduce-window(s32[64,8,128]{2,1,0:T(8,128)S(1)} %fusion.97, s32[]{:T(128)} %constant.30.clone.1), window={size=1x1x128 pad=0_0x0_0x127_0}, to_apply=%region_6.7 | reduce-window | flops 8323072 | bytes 524292 | tf_op jit(solution)/shard_map/reduce-window
  128.0 130.4 %reduce-scatter.2.cloned.1.call-done = f32[128,2048]{1,0:T(8,128)} async-done(((f32[1024,2048]{1,0:T(8,128)}), f32[128,2048]{1,0:T(8,128)}) %reduce-scatter.2.cloned.1.call-update) | async-done | bytes 1048592 | tf_op jit(solution)/shard_map/reduce_scatter | solution.py:70
  262.0 9.9 scatter_custom_fusion
  271.9 8.9 reshape.129
  294.0 23.7 %reshape_reshape.3 = bf16[32,4,20,2048]{3,1,0,2:T(4,128)(2,1)} reshape(bf16[64,2,20,2048]{3,1,0,2:T(2,128)(2,1)} %broadcast_in_dim.54) | data formatting | bytes 20971520 | tf_op jit(solution)/shard_map/reshape;reshape | solution.py:98
  324.8 233.5 %all_to_all.10 = bf16[32,4,20,2048]{3,1,2,0:T(4,128)(2,1)} all-to-all(bf16[32,4,20,2048]{3,1,2,0:T(4,128)(2,1)S(1)} %copy.91), channel_id=1, replica_groups=mesh['req'=4,'exp'=8] {'req','exp'}, dimensions={0} | all-to-all | bytes 20971520 | tf_op jit(solution)/shard_map/all_to_all | solution.py:99
  558.3 56.3 %slice_reduce_fusion.3 = (bf16[32,20,2048]{2,1,0:T(8,128)(2,1)}, bf16[32,20,2048]{2,1,0:T(8,128)(2,1)}, bf16[32,20,2048]{2,1,0:T(8,128)(2,1)}, bf16[32,20,2048]{2,1,0:T(8,128)(2,1)}) fusion(bf16[32,4,20,2048]{3,1,2,0:T(4,128)(2,1)} %all_to_all.10), kind=kLoop, calls=%fused_computation.32 | loop fusion | bytes 20971520 | tf_op jit(solution)/shard_map/slice | solution.py:105
  623.7 7.5 convolution_convert_fusion
  667.7 7.5 convolution_convert_fusion.2
  689.5 7.5 convolution_convert_fusion.3
  709.4 23.6 %copy.92 = bf16[32,4,20,2048]{3,1,2,0:T(4,128)(2,1)} copy(bf16[32,4,20,2048]{3,2,0,1:T(8,128)(2,1)S(1)} %pad_maximum_fusion) | data formatting | bytes 20971520 | tf_op jit(solution)/shard_map/stack | solution.py:118
  737.0 232.2 %all-to-all-done.1 = bf16[32,4,20,2048]{3,1,2,0:T(4,128)(2,1)} async-done(((bf16[32,4,20,2048]{3,1,2,0:T(4,128)(2,1)}), bf16[32,4,20,2048]{3,1,2,0:T(4,128)(2,1)}, u32[]{:S(2)}, u32[]{:S(2)}) %all-to-all-start.1) | async-done | bytes 10485792 | tf_op jit(solution)/shard_map/all_to_all | solution.py:117
  969.1 9.9 copy.93
  979.0 21.7 %reshape.130 = bf16[64,2,20,2048]{3,1,0,2:T(2,128)(2,1)} reshape(bf16[32,4,20,2048]{3,1,0,2:T(4,128)(2,1)} %copy.93) | data formatting | bytes 20971520 | tf_op jit(solution)/shard_map/reshape | solution.py:120
  1000.7 21.5 %fusion.104 = (bf16[64,1,20,2048]{3,1,0,2:T(2,128)(2,1)}, bf16[64,1,20,2048]{3,1,0,2:T(2,128)(2,1)}) fusion(bf16[64,2,20,2048]{3,1,0,2:T(2,128)(2,1)} %reshape.130), kind=kLoop, calls=%fused_computation.103 | loop fusion | bytes 20971520 | tf_op jit(solution)/shard_map/slice | solution.py:121
  1022.2 21.5 %convert_add_fusion = f32[64,1,20,2048]{3,0,2,1:T(8,128)} fusion(bf16[64,1,20,2048]{3,1,0,2:T(2,128)(2,1)} %get-tuple-element.90, bf16[64,1,20,2048]{3,1,0,2:T(2,128)(2,1)} %get-tuple-element.89), kind=kLoop, calls=%fused_computation.26 | loop fusion | flops 7864320 | bytes 20971520 | tf_op jit(solution)/shard_map/add | solution.py:121
  1043.7 14.9 %copy.96 = f32[64,1,20,2048]{3,2,0,1:T(8,128)} copy(f32[64,1,20,2048]{3,0,2,1:T(8,128)} %convert_add_fusion) | data formatting | bytes 20971520 | tf_op jit(solution)/shard_map/add | solution.py:121
  1058.7 12.7 %add.79 = f32[1280,2048]{1,0:T(8,128)} reshape(f32[64,1,20,2048]{3,2,0,1:T(8,128)} %copy.96) | data formatting | bytes 20971520 | tf_op jit(solution)/shard_map/add | solution.py:121
  1071.4 13.1 %gather_fusion = f32[1024,2048]{1,0:T(8,128)} fusion(f32[1280,2048]{1,0:T(8,128)} %add.79, s32[1024]{0:T(1024)S(1)} %broadcast_clamp_fusion), kind=kCustom, calls=%fused_computation | custom fusion | bytes 16781312 | tf_op jit(solution)/shard_map/gather | solution.py:124
  (92 shorter events, 174.1 us)
Async XLA Ops:
  7.2 95.4 %copy-start = (bf16[256,2048]{1,0:T(8,128)(2,1)S(1)}, bf16[256,2048]{1,0:T(8,128)(2,1)}, u32[]{:S(2)}) copy-start(bf16[256,2048]{1,0:T(8,128)(2,1)} %param.17) | copy-start | bytes 3145732
  7.2 251.2 %reduce-scatter.2.cloned.1.call-start = ((), (), s32[]{:S(2)}) async-start(), calls=%async_computation.3 | async-start | bytes 9437184 | tf_op jit(solution)/shard_map/reduce_scatter | solution.py:70
  17.2 4.1 copy-start.6
  64.9 4.1 copy-start.6
  108.1 0.7 copy-start.3
  108.8 149.6 %copy-start.2 = (bf16[128,2048]{1,0:T(8,128)(2,1)S(1)}, bf16[128,2048]{1,0:T(8,128)(2,1)}, u32[]{:S(2)}) copy-start(bf16[128,2048]{1,0:T(8,128)(2,1)} %param.18) | copy-start | bytes 1572868
  108.8 151.1 %copy-start.4 = (f32[2048]{0:T(1024)S(1)}, f32[2048]{0:T(1024)}, u32[]{:S(2)}) copy-start(f32[2048]{0:T(1024)} %param.19) | copy-start | bytes 24580
  733.0 3.8 copy-start.5
  733.0 236.1 %all-to-all-start.1 = ((bf16[32,4,20,2048]{3,1,2,0:T(4,128)(2,1)}), bf16[32,4,20,2048]{3,1,2,0:T(4,128)(2,1)}, u32[]{:S(2)}, u32[]{:S(2)}) async-start(bf16[32,4,20,2048]{3,1,2,0:T(4,128)(2,1)} %copy.92), calls=%async_computation.2 | async-start | bytes 20971520 | tf_op jit(solution)/shard_map/all_to_all | solution.py:117
  1071.4 20.4 %copy-start.1 = (bf16[256,2048]{1,0:T(8,128)(2,1)S(1)}, bf16[256,2048]{1,0:T(8,128)(2,1)}, u32[]{:S(2)}) copy-start(bf16[256,2048]{1,0:T(8,128)(2,1)} %param.17) | copy-start | bytes 3145732
Sparse Core Ops, SparseCore 0:
  108.2 150.0 reduce-scatter.1
where the time goes:
time: 1110 us; the launch traced here: 1100 us
  waiting for transfers between devices  363 us (33%)
  local copies, waits for them, and re-layouts  320 us (29%)
  blocking collectives  234 us (21%)
  matrix products  90.2 us (8%)
  other arithmetic  74.2 us (7%)
  between operations  14.4 us (1%)
    all_to_all x1, blocking collectives, local(): lax.all_to_all(outgoing, ('req', 'exp'), split_axis=0, concat_axis=0, til...  234 us
    all_to_all x1, waiting for transfers between devices, local(): lax.all_to_all(jnp.stack(outputs, axis=1), ('req', 'exp'), split_axis=0,...  232 us
    reduce_scatter x1, waiting for transfers between devices, local(): lax.psum_scatter(jnp.dot(attention, out_proj, preferred_element_type=jnp....  130 us
    slice x1, local copies, waits for them, and re-layouts, local(): rows = arrived[:, piece_index].reshape(sources * items, model_width)  56.3 us
    another operation x5, local copies, waits for them, and re-layouts, local(): jnp.stack(outputs, axis=1)  44.3 us
    another operation x2, local copies, waits for them, and re-layouts, local(): outgoing = outgoing.reshape(devices, pieces, capacity, model_width)  30.8 us
    dot_general x4, matrix products, local(): jnp.dot(inner, expert_down[lower:lower + half_units], preferred_element_t...  30.1 us
    add x2, local copies, waits for them, and re-layouts, local(): halves[:, 0].astype(jnp.float32) + halves[:, 1].astype(jnp.float32)  27.6 us
  transfers between devices with their start and end apart: 2, of which 2 were waited for; matrix products, arithmetic and copies ran while one was open for 2% of the time, Pallas kernels for 0%

commit v1 on v0

--- a/solution.py
+++ b/solution.py
@@ -27,6 +27,8 @@
     cache_len = cache_entries.shape[2]
     tok_local = residual.shape[0]
     model_width = residual.shape[1]
+
+    full_proj = lax.all_gather(out_proj, "exp", axis=0, tiled=True)
 
     def attend_request(packed):
         query_rows, new_rows, cache_rows, length = packed
@@ -67,62 +69,65 @@
 
     attention = lax.map(attend_request, (queries, new_entries, cache_entries, cache_lengths))
     attention = attention.reshape(req_local * new_len, width_local)
-    projected = lax.psum_scatter(
-        jnp.dot(attention, out_proj, preferred_element_type=jnp.float32),
-        "exp",
-        scatter_dimension=0,
-        tiled=True,
-    )
+    features = lax.all_to_all(attention, "exp", split_axis=0, concat_axis=1, tiled=True)
+    projected = jnp.dot(features, full_proj, preferred_element_type=jnp.float32)
     hidden = residual.astype(jnp.float32) + projected
     attended = hidden.astype(jnp.bfloat16)
     mean_square = jnp.mean(hidden * hidden, axis=-1, keepdims=True)
     normed = (hidden * lax.rsqrt(mean_square + 1e-05) * norm_gain).astype(jnp.bfloat16)
-    req_count = lax.axis_size("req")
-    exp_count = lax.axis_size("exp")
-    devices = req_count * exp_count
-    half_units = FF // 2
-    pieces = expert_in.shape[2] // half_units
+    devices = lax.axis_size("req") * lax.axis_size("exp")
+    width_units = expert_in.shape[2]
+    copies = max(1, FF // width_units)
+    experts_local = max(1, width_units // FF)
     capacity = max(2, tok_local * TOP * 5 // (EXPERTS * 4))
-    flat_routes = routes.reshape(-1)
-    onehot = (flat_routes[:, None] == jnp.arange(EXPERTS, dtype=jnp.int32)[None, :]).astype(
-        jnp.int32
-    )
-    slot_index = jnp.sum(jnp.cumsum(onehot, axis=0) * onehot, axis=1) - 1
-    positions = flat_routes * capacity + slot_index
-    slot_rows = (
-        jnp.zeros((EXPERTS * capacity, model_width), jnp.bfloat16)
-        .at[positions]
-        .set(jnp.repeat(normed, TOP, axis=0))
-    )
-    outgoing = jnp.repeat(slot_rows.reshape(EXPERTS, capacity, model_width), 2, axis=0)
-    outgoing = outgoing.reshape(devices, pieces, capacity, model_width)
+    slots = EXPERTS * copies * capacity
+    onehot = routes[:, :, None] == jnp.arange(EXPERTS, dtype=jnp.int32)[None, None, :]
+    chosen = jnp.any(onehot, axis=1).astype(jnp.bfloat16)
+    token_ids = jnp.arange(tok_local, dtype=jnp.int32)
+    earlier = (token_ids[None, :] < token_ids[:, None]).astype(jnp.bfloat16)
+    rank = jnp.dot(earlier, chosen, preferred_element_type=jnp.float32).astype(jnp.int32)
+    slot_index = jnp.sum(jnp.where(onehot, rank[:, None, :], 0), axis=2)
+    positions = routes * capacity + slot_index
+    slot_ids = jnp.arange(slots, dtype=jnp.int32)
+    slot_keys = slot_ids // (copies * capacity) * capacity + slot_ids % capacity
+    places = jnp.transpose(positions)
+    fill = jnp.zeros((slots, tok_local), jnp.bool_)
+    mix = jnp.zeros((tok_local, slots), jnp.float32)
+    for choice in range(TOP):
+        fill = fill | (slot_keys[:, None] == places[choice][None, :])
+        mix = mix + jnp.where(
+            positions[:, choice][:, None] == slot_keys[None, :],
+            gate_weights[:, choice][:, None],
+            0.0,
+        )
+    outgoing = jnp.dot(
+        fill.astype(jnp.bfloat16), normed, preferred_element_type=jnp.float32
+    ).astype(jnp.bfloat16)
+    items = experts_local * capacity
+    outgoing = outgoing.reshape(devices, items, model_width)
     arrived = lax.all_to_all(outgoing, ("req", "exp"), split_axis=0, concat_axis=0, tiled=True)
-    sources = arrived.shape[0]
-    items = arrived.shape[2]
-    outputs = []
-    for piece_index in range(pieces):
-        lower = piece_index * half_units
-        rows = arrived[:, piece_index].reshape(sources * items, model_width)
-        gate_part = jnp.dot(
-            rows, expert_in[0, :, lower : lower + half_units], preferred_element_type=jnp.float32
-        )
-        up_part = jnp.dot(
-            rows, expert_in[1, :, lower : lower + half_units], preferred_element_type=jnp.float32
-        )
-        inner = (jax.nn.silu(gate_part) * up_part).astype(jnp.bfloat16)
-        half_out = jnp.dot(
-            inner, expert_down[lower : lower + half_units], preferred_element_type=jnp.float32
-        ).astype(jnp.bfloat16)
-        outputs.append(half_out.reshape(sources, items, model_width))
+    rows = arrived.reshape(devices * items, model_width)
+    gate_part = jnp.dot(rows, expert_in[0], preferred_element_type=jnp.float32)
+    up_part = jnp.dot(rows, expert_in[1], preferred_element_type=jnp.float32)
+    row_expert = jnp.arange(devices * items, dtype=jnp.int32) % items // capacity
+    unit_expert = jnp.arange(width_units, dtype=jnp.int32) // FF
+    own = row_expert[:, None] == unit_expert[None, :]
+    inner = jnp.where(own, jax.nn.silu(gate_part) * up_part, 0.0).astype(jnp.bfloat16)
+    outputs = jnp.dot(inner, expert_down, preferred_element_type=jnp.float32).astype(jnp.bfloat16)
     returned = lax.all_to_all(
-        jnp.stack(outputs, axis=1), ("req", "exp"), split_axis=0, concat_axis=0, tiled=True
-    )
-    halves = returned.reshape(EXPERTS, 2, capacity, model_width)
-    summed = (halves[:, 0].astype(jnp.float32) + halves[:, 1].astype(jnp.float32)).reshape(
-        EXPERTS * capacity, model_width
-    )
-    picked = summed[positions] * gate_weights.reshape(-1)[:, None]
-    expert_out = jnp.sum(picked.reshape(tok_local, TOP, model_width), axis=1).astype(jnp.bfloat16)
+        outputs.reshape(devices, items, model_width),
+        ("req", "exp"),
+        split_axis=0,
+        concat_axis=0,
+        tiled=True,
+    ).reshape(slots, model_width)
+    first = lax.reduce_precision(mix, 8, 7)
+    second = lax.reduce_precision(mix - first, 8, 7)
+    third = mix - first - second
+    terms = jnp.concatenate([first, second, third], axis=0).astype(jnp.bfloat16)
+    mixed = jnp.dot(terms, returned, preferred_element_type=jnp.float32)
+    mixed = mixed.reshape(3, tok_local, model_width)
+    expert_out = (mixed[0] + mixed[1] + mixed[2]).astype(jnp.bfloat16)
     return (attended, expert_out)
 
 

time: 1110 us -> 462 us (0.42)
  local copies, waits for them, and re-layouts: 320 us -> 26.5 us
  blocking collectives: 234 us -> 0 us
  waiting for transfers between devices: 363 us -> 284 us
  other arithmetic: 74.2 us -> 19.8 us
  matrix products: 90.2 us -> 102 us
  starting transfers between devices: 3.87 us -> 15 us
    all_to_all x1 -> x0, blocking collectives: 234 us -> none  [local(): lax.all_to_all(outgoing, ('req', 'exp'), split_axis=0, concat_axis=0, til...]
    reduce_scatter x1 -> x0, waiting for transfers between devices: 130 us -> none  [local(): lax.psum_scatter(jnp.dot(attention, out_proj, preferred_element_type=jnp....]
    another operation x13 -> x0, local copies, waits for them, and re-layouts: 96.3 us -> none  [the longest x5 44.3 us: local(): jnp.stack(outputs, axis=1)]
    slice x4 -> x0, local copies, waits for them, and re-layouts: 78 us -> none  [the longest x1 56.3 us: local(): rows = arrived[:, piece_index].reshape(sources * items, model_width)]
    reshape x3 -> x0, local copies, waits for them, and re-layouts: 36.3 us -> none  [the longest x1 21.7 us: local(): halves = returned.reshape(EXPERTS, 2, capacity, model_width)]
    all_to_all x1 -> x3, waiting for transfers between devices: 232 us -> 263 us  [the longest x1 117 us: local(): lax.all_to_all(outgoing, ('req', 'exp'), split_axis=0, concat_axis=0, til...]
    add x2 -> x0, local copies, waits for them, and re-layouts: 27.6 us -> none  [local(): halves[:, 0].astype(jnp.float32) + halves[:, 1].astype(jnp.float32)]
    another operation x4 -> x1, other arithmetic: 25.4 us -> 0.68 us
  transfers between devices with their start and end apart: 2 -> 4, of which waited for: 2 -> 4; matrix products, arithmetic and copies ran while one was open for 2% -> 18% of each run, Pallas kernels for 0% -> 0%
where the time goes in v1:
time: 462 us; the launch traced here: 461 us
  waiting for transfers between devices  284 us (61%)
  matrix products  102 us (22%)
  local copies, waits for them, and re-layouts  26.5 us (6%)
  other arithmetic  19.8 us (4%)
  starting transfers between devices  15 us (3%)
  between operations  14.2 us (3%)
    all_to_all x1, waiting for transfers between devices, local(): lax.all_to_all(outgoing, ('req', 'exp'), split_axis=0, concat_axis=0, til...  117 us
    all_to_all x1, waiting for transfers between devices, local(): lax.all_to_all(outputs.reshape(devices, items, model_width), ('req', 'exp...  117 us
    dot_general x1, matrix products, local(): jnp.dot(inner, expert_down, preferred_element_type=jnp.float32)  32.3 us
    all_to_all x1, waiting for transfers between devices, local(): lax.all_to_all(attention, 'exp', split_axis=0, concat_axis=1, tiled=True)  29.1 us
    all_gather x1, waiting for transfers between devices, local(): full_proj = lax.all_gather(out_proj, 'exp', axis=0, tiled=True)  19.4 us
    dot_general x2, matrix products, attend_request(): jnp.einsum('thd,jhd->htj', query_heads, cache_keys, preferred_element_typ...  18.9 us
    dot_general x2, matrix products, attend_request(): jnp.einsum('htj,jhd->thd', weights_bf, all_vals, preferred_element_type=j...  17.9 us
    dot_general x1, matrix products, local(): gate_part = jnp.dot(rows, expert_in[0], preferred_element_type=jnp.float32)  17.4 us
  transfers between devices with their start and end apart: 4, of which 4 were waited for; matrix products, arithmetic and copies ran while one was open for 18% of the time, Pallas kernels for 0%

profile of v1, /device:TPU:0, one launch (start us, length us, event | category | flops | bytes accessed | tf_op | source)
XLA Modules:
  0.0 461.1 jit_solution(8890040560525605997)
XLA Ops:
  7.9 82.6 %while.10 = (s32[]{:T(128)}, bf16[2,512,256]{2,1,0:T(8,128)(2,1)}, bf16[2,2,4096,256]{3,2,1,0:T(8,128)(2,1)}, bf16[2,2,512,256]{3,2,1,0:T(8,128)(2,1)}, s32[2]{0...) while((s32[]{:T(128)}, bf16[2,512,256]{2,1,0:T(8,128)(2,1)}, ...), condition=%wide.region_4.5_spmd, body=%wide.region_0.4_spmd.sunk | while | flops 2463631360 | bytes 102543704 | solution.py:70
  8.0 3.9 constant_dynamic-slice_fusion.10
  11.8 4.1 copy.62
  17.4 9.2 %fusion.124 = (f32[2,512]{1,0:T(2,128)S(1)}, f32[2,512,4096]{2,1,0:T(8,128)}) fusion(bf16[512,2,128]{0,2,1:T(8,128)(2,1)S(1)} %bitcast.117, bf16[4096,2,128]{0,2,1:T(8,128)(2,1)} %bitcast.116, pred[4096]{0:T(1024)(128)(4,1)S(1)} %iota_compare_fusion.8), kind=kOutput, calls=%fused_computation.143.clone.1 | convolution fusion | flops 1086323712 | bytes 19144704 | tf_op jit(solution)/shard_map/while/body/eval_jaxpr/thd,jhd->htj/dot_general | solution.py:42
  27.6 8.3 %fusion.125 = f32[2,512]{1,0:T(2,128)S(1)} fusion(f32[2,512,512]{2,1,0:T(8,128)S(1)} %get-tuple-element.149, f32[2,512,4096]{2,1,0:T(8,128)} %get-tuple-element.151, f32[2,512]{1,0:T(2,128)S(1)} %reduce_max.27), kind=kLoop, calls=%fused_computation.3.clone.1 | loop fusion | flops 14154752 | bytes 18882560 | tf_op jit(solution)/shard_map/while/body/eval_jaxpr/reduce_sum | solution.py:63
  35.8 3.0 copy.64
  39.0 9.0 %fusion.126 = bf16[512,2,128]{0,2,1:T(8,128)(2,1)S(1)} fusion(f32[2,512,512]{2,1,0:T(8,128)} %copy-done, f32[2,512,4096]{2,1,0:T(8,128)} %get-tuple-element.151, f32[2,512]{1,0:T(2,128)S(1)} %reduce_max.27, bf16[512,2,128]{0,2,1:T(8,128)(2,1)S(1)} %bitcast.122, bf16[4096,2,128]{0,2,1:T(8,128)(2,1)} %bitcast.119, f32[512,2]{0,1:T(2,128)S(1)} %bitcast.128), kind=kOutput, calls=%fused_computation.13.clone.1 | convolution fusion | flops 1227096064 | bytes 21504000 | tf_op jit(solution)/shard_map/while/body/eval_jaxpr/htj,jhd->thd/dot_general | solution.py:66
  49.0 3.9 constant_dynamic-slice_fusion.10
  52.9 4.1 copy.62
  58.4 9.7 %fusion.124 = (f32[2,512]{1,0:T(2,128)S(1)}, f32[2,512,4096]{2,1,0:T(8,128)}) fusion(bf16[512,2,128]{0,2,1:T(8,128)(2,1)S(1)} %bitcast.117, bf16[4096,2,128]{0,2,1:T(8,128)(2,1)} %bitcast.116, pred[4096]{0:T(1024)(128)(4,1)S(1)} %iota_compare_fusion.8), kind=kOutput, calls=%fused_computation.143.clone.1 | convolution fusion | flops 1086323712 | bytes 19144704 | tf_op jit(solution)/shard_map/while/body/eval_jaxpr/thd,jhd->htj/dot_general | solution.py:42
  69.1 8.3 %fusion.125 = f32[2,512]{1,0:T(2,128)S(1)} fusion(f32[2,512,512]{2,1,0:T(8,128)S(1)} %get-tuple-element.149, f32[2,512,4096]{2,1,0:T(8,128)} %get-tuple-element.151, f32[2,512]{1,0:T(2,128)S(1)} %reduce_max.27), kind=kLoop, calls=%fused_computation.3.clone.1 | loop fusion | flops 14154752 | bytes 18882560 | tf_op jit(solution)/shard_map/while/body/eval_jaxpr/reduce_sum | solution.py:63
  80.6 8.9 %fusion.126 = bf16[512,2,128]{0,2,1:T(8,128)(2,1)S(1)} fusion(f32[2,512,512]{2,1,0:T(8,128)} %copy-done, f32[2,512,4096]{2,1,0:T(8,128)} %get-tuple-element.151, f32[2,512]{1,0:T(2,128)S(1)} %reduce_max.27, bf16[512,2,128]{0,2,1:T(8,128)(2,1)S(1)} %bitcast.122, bf16[4096,2,128]{0,2,1:T(8,128)(2,1)} %bitcast.119, f32[512,2]{0,1:T(2,128)S(1)} %bitcast.128), kind=kOutput, calls=%fused_computation.13.clone.1 | convolution fusion | flops 1227096064 | bytes 21504000 | tf_op jit(solution)/shard_map/while/body/eval_jaxpr/htj,jhd->thd/dot_general | solution.py:66
  90.5 7.3 %all-to-all-start = ((bf16[8,128,256]{2,1,0:T(8,128)(2,1)}), bf16[8,128,256]{2,1,0:T(8,128)(2,1)S(1)}, u32[]{:S(2)}, u32[]{:S(2)}) async-start(bf16[8,128,256]{2,1,0:T(8,128)(2,1)} %bitcast.127), calls=%async_computation | async-start | bytes 1048576 | tf_op jit(solution)/shard_map/all_to_all | solution.py:72
  98.1 29.1 %all-to-all-done = bf16[8,128,256]{2,1,0:T(8,128)(2,1)S(1)} async-done(((bf16[8,128,256]{2,1,0:T(8,128)(2,1)}), bf16[8,128,256]{2,1,0:T(8,128)(2,1)S(1)}, u32[]{:S(2)}, u32[]{:S(2)}) %all-to-all-start) | async-done | bytes 524320 | tf_op jit(solution)/shard_map/all_to_all | solution.py:72
  127.5 19.4 %all-gather.2.cloned.1.call-done = bf16[2048,2048]{1,0:T(8,128)(2,1)} async-done(((bf16[256,2048]{1,0:T(8,128)(2,1)}), bf16[2048,2048]{1,0:T(8,128)(2,1)}) %all-gather.2.cloned.1.call-update) | async-done | bytes 8388624 | tf_op jit(solution)/shard_map/all_gather | solution.py:31
  146.9 5.5 %multiply_reduce_fusion = (f32[128]{0:T(128)S(1)}, bf16[128,2048]{1,0:T(8,128)(2,1)}, f32[128,2048]{1,0:T(8,128)S(1)}) fusion(bf16[128,2048]{0,1:T(8,128)(2,1)S(1)} %bitcast.125, bf16[2048,2048]{1,0:T(8,128)(2,1)} %all-gather.2.cloned.1.call-done, bf16[128,2048]{1,0:T(8,128)(2,1)} %param.18), kind=kOutput, calls=%fused_computation.42 | convolution fusion | flops 1075052416 | bytes 11010560 | tf_op jit(solution)/shard_map/dot_general | solution.py:73
  152.5 3.6 convolution_convert_fusion
  156.1 3.9 all-to-all-start.1
  160.1 117.4 %all-to-all-done.1 = bf16[32,40,2048]{2,1,0:T(8,128)(2,1)} async-done(((bf16[32,40,2048]{2,1,0:T(8,128)(2,1)}), bf16[32,40,2048]{2,1,0:T(8,128)(2,1)}, u32[]{:S(2)}, u32[]{:S(2)}) %all-to-all-start.1) | async-done | bytes 5242912 | tf_op jit(solution)/shard_map/all_to_all | solution.py:108
  277.5 17.4 %fusion.28 = f32[1280,2048]{1,0:T(8,128)} fusion(bf16[1280,2048]{1,0:T(8,128)(2,1)} %bitcast.38, bf16[2,2048,2048]{2,1,0:T(8,128)(2,1)} %param.22), kind=kOutput, calls=%fused_computation.26 | convolution fusion | flops 10737418240 | bytes 24117248 | tf_op jit(solution)/shard_map/dot_general | solution.py:110
  294.8 32.3 %fusion.33 = bf16[1280,2048]{1,0:T(8,128)(2,1)} fusion(bf16[2048,2048]{1,0:T(8,128)(2,1)} %param.23, f32[1280,2048]{1,0:T(8,128)} %fusion.28, bf16[1280,2048]{1,0:T(8,128)(2,1)} %bitcast.38, bf16[2,2048,2048]{2,1,0:T(8,128)(2,1)} %param.22, s32[2048]{0:T(1024)S(1)} %add_select_fusion, s32[1280]{0:T(1024)S(1)} %add_select_fusion.1), kind=kOutput, calls=%fused_computation.30 | convolution fusion | flops 21498429440 | bytes 37762048 | tf_op jit(solution)/shard_map/dot_general | solution.py:116
  327.2 3.7 all-to-all-start.2
  331.7 116.9 %all-to-all-done.2 = bf16[32,40,2048]{2,1,0:T(8,128)(2,1)} async-done(((bf16[32,40,2048]{2,1,0:T(8,128)(2,1)}), bf16[32,40,2048]{2,1,0:T(8,128)(2,1)}, u32[]{:S(2)}, u32[]{:S(2)}) %all-to-all-start.2) | async-done | bytes 5242912 | tf_op jit(solution)/shard_map/all_to_all | solution.py:117
  448.6 4.7 %fusion.41 = f32[384,2048]{1,0:T(8,128)S(1)} fusion(bf16[1280,2048]{1,0:T(8,128)(2,1)} %bitcast.42, bf16[128,1280]{1,0:T(8,128)(2,1)S(1)} %get-tuple-element.77, bf16[128,1280]{1,0:T(8,128)(2,1)S(1)} %get-tuple-element.76, bf16[128,1280]{1,0:T(8,128)(2,1)S(1)} %get-tuple-element.75), kind=kOutput, calls=%fused_computation.43 | convolution fusion | flops 2016215040 | bytes 9371648 | tf_op jit(solution)/shard_map/dot_general | solution.py:128
  (80 shorter events, 12.9 us)
Async XLA Ops:
  7.2 139.7 %all-gather.2.cloned.1.call-start = ((), (), s32[]{:S(2)}) async-start(), calls=%async_computation.3 | async-start | bytes 9437184 | tf_op jit(solution)/shard_map/all_gather | solution.py:31
  7.9 89.9 %copy-start.7 = (s32[128,8]{0,1:T(8,128)S(1)}, s32[128,8]{0,1:T(8,128)}, u32[]{:S(2)}) copy-start(s32[128,8]{0,1:T(8,128)} %param.20) | copy-start | bytes 12292
  7.9 8.0 %copy-start.2 = (bf16[2,512,256]{2,1,0:T(8,128)(2,1)S(1)}, bf16[2,512,256]{2,1,0:T(8,128)(2,1)}, u32[]{:S(2)}) copy-start(bf16[2,512,256]{2,1,0:T(8,128)(2,1)} %get-tuple-element.179) | copy-start | bytes 1572868 | tf_op jit(solution)/shard_map/while
  7.9 8.2 %copy-start.12 = (s32[2]{0:T(128)S(1)}, s32[2]{0:T(128)}, u32[]{:S(2)}) copy-start(s32[2]{0:T(128)} %get-tuple-element.178) | copy-start | bytes 28 | tf_op jit(solution)/shard_map/while
  17.4 9.2 %copy-start.1 = (bf16[2,2,512,256]{3,2,1,0:T(8,128)(2,1)S(1)}, bf16[2,2,512,256]{3,2,1,0:T(8,128)(2,1)}, u32[]{:S(2)}) copy-start(bf16[2,2,512,256]{3,2,1,0:T(8,128)(2,1)} %get-tuple-element.177) | copy-start | bytes 3145732 | tf_op jit(solution)/shard_map/while
  27.5 8.3 %copy-start = (f32[2,512,512]{2,1,0:T(8,128)}, f32[2,512,512]{2,1,0:T(8,128)S(1)}, u32[]{:S(2)}) copy-start(f32[2,512,512]{2,1,0:T(8,128)S(1)} %get-tuple-element.149) | copy-start | bytes 6291460 | tf_op jit(solution)/shard_map/while
  39.0 9.1 %copy-start.3 = (bf16[2,512,256]{2,1,0:T(8,128)(2,1)S(1)}, bf16[2,512,256]{2,1,0:T(8,128)(2,1)}, u32[]{:S(2)}) copy-start(bf16[2,512,256]{2,1,0:T(8,128)(2,1)} %get-tuple-element.166) | copy-start | bytes 1572868 | tf_op jit(solution)/shard_map/while
  48.2 0.8 copy-start.4
  49.0 8.0 %copy-start.2 = (bf16[2,512,256]{2,1,0:T(8,128)(2,1)S(1)}, bf16[2,512,256]{2,1,0:T(8,128)(2,1)}, u32[]{:S(2)}) copy-start(bf16[2,512,256]{2,1,0:T(8,128)(2,1)} %get-tuple-element.179) | copy-start | bytes 1572868 | tf_op jit(solution)/shard_map/while
  49.0 8.2 %copy-start.12 = (s32[2]{0:T(128)S(1)}, s32[2]{0:T(128)}, u32[]{:S(2)}) copy-start(s32[2]{0:T(128)} %get-tuple-element.178) | copy-start | bytes 28 | tf_op jit(solution)/shard_map/while
  58.4 9.7 %copy-start.1 = (bf16[2,2,512,256]{3,2,1,0:T(8,128)(2,1)S(1)}, bf16[2,2,512,256]{3,2,1,0:T(8,128)(2,1)}, u32[]{:S(2)}) copy-start(bf16[2,2,512,256]{3,2,1,0:T(8,128)(2,1)} %get-tuple-element.177) | copy-start | bytes 3145732 | tf_op jit(solution)/shard_map/while
  69.1 8.3 %copy-start = (f32[2,512,512]{2,1,0:T(8,128)}, f32[2,512,512]{2,1,0:T(8,128)S(1)}, u32[]{:S(2)}) copy-start(f32[2,512,512]{2,1,0:T(8,128)S(1)} %get-tuple-element.149) | copy-start | bytes 6291460 | tf_op jit(solution)/shard_map/while
  80.6 9.1 %copy-start.3 = (bf16[2,512,256]{2,1,0:T(8,128)(2,1)S(1)}, bf16[2,512,256]{2,1,0:T(8,128)(2,1)}, u32[]{:S(2)}) copy-start(bf16[2,512,256]{2,1,0:T(8,128)(2,1)} %get-tuple-element.166) | copy-start | bytes 1572868 | tf_op jit(solution)/shard_map/while
  89.7 0.8 copy-start.4
  90.5 36.7 %all-to-all-start = ((bf16[8,128,256]{2,1,0:T(8,128)(2,1)}), bf16[8,128,256]{2,1,0:T(8,128)(2,1)S(1)}, u32[]{:S(2)}, u32[]{:S(2)}) async-start(bf16[8,128,256]{2,1,0:T(8,128)(2,1)} %bitcast.127), calls=%async_computation | async-start | bytes 1048576 | tf_op jit(solution)/shard_map/all_to_all | solution.py:72
  97.8 54.6 %copy-start.5 = (s32[1280]{0:T(1024)}, s32[1280]{0:T(1024)S(1)}, u32[]{:S(2)}) copy-start(s32[1280]{0:T(1024)S(1)} %fusion.82) | copy-start | bytes 15364
  98.1 54.4 %copy-start.8 = (s32[128,8]{0,1:T(8,128)}, s32[128,8]{0,1:T(8,128)S(1)}, u32[]{:S(2)}) copy-start(s32[128,8]{0,1:T(8,128)S(1)} %multiply_add_fusion) | copy-start | bytes 12292
  146.9 5.6 %copy-start.10 = (f32[2048]{0:T(1024)S(1)}, f32[2048]{0:T(1024)}, u32[]{:S(2)}) copy-start(f32[2048]{0:T(1024)} %param.19) | copy-start | bytes 24580
  156.1 121.4 %all-to-all-start.1 = ((bf16[32,40,2048]{2,1,0:T(8,128)(2,1)}), bf16[32,40,2048]{2,1,0:T(8,128)(2,1)}, u32[]{:S(2)}, u32[]{:S(2)}) async-start(bf16[32,40,2048]{2,1,0:T(8,128)(2,1)} %bitcast.120), calls=%async_computation.1 | async-start | bytes 10485760 | tf_op jit(solution)/shard_map/all_to_all | solution.py:108
  327.2 3.8 copy-start.9
  327.2 3.8 copy-start.11
  327.2 3.8 copy-start.6
  327.2 121.4 %all-to-all-start.2 = ((bf16[32,40,2048]{2,1,0:T(8,128)(2,1)}), bf16[32,40,2048]{2,1,0:T(8,128)(2,1)}, u32[]{:S(2)}, u32[]{:S(2)}) async-start(bf16[32,40,2048]{2,1,0:T(8,128)(2,1)} %bitcast.124), calls=%async_computation.2 | async-start | bytes 10485760 | tf_op jit(solution)/shard_map/all_to_all | solution.py:117
Sparse Core Ops, SparseCore 0:
  10.1 136.7 all-gather.1

commit v2 on v1

--- a/solution.py
+++ b/solution.py
@@ -80,7 +80,6 @@
     copies = max(1, FF // width_units)
     experts_local = max(1, width_units // FF)
     capacity = max(2, tok_local * TOP * 5 // (EXPERTS * 4))
-    slots = EXPERTS * copies * capacity
     onehot = routes[:, :, None] == jnp.arange(EXPERTS, dtype=jnp.int32)[None, None, :]
     chosen = jnp.any(onehot, axis=1).astype(jnp.bfloat16)
     token_ids = jnp.arange(tok_local, dtype=jnp.int32)
@@ -88,46 +87,71 @@
     rank = jnp.dot(earlier, chosen, preferred_element_type=jnp.float32).astype(jnp.int32)
     slot_index = jnp.sum(jnp.where(onehot, rank[:, None, :], 0), axis=2)
     positions = routes * capacity + slot_index
-    slot_ids = jnp.arange(slots, dtype=jnp.int32)
-    slot_keys = slot_ids // (copies * capacity) * capacity + slot_ids % capacity
     places = jnp.transpose(positions)
-    fill = jnp.zeros((slots, tok_local), jnp.bool_)
-    mix = jnp.zeros((tok_local, slots), jnp.float32)
-    for choice in range(TOP):
-        fill = fill | (slot_keys[:, None] == places[choice][None, :])
-        mix = mix + jnp.where(
-            positions[:, choice][:, None] == slot_keys[None, :],
-            gate_weights[:, choice][:, None],
-            0.0,
-        )
-    outgoing = jnp.dot(
-        fill.astype(jnp.bfloat16), normed, preferred_element_type=jnp.float32
-    ).astype(jnp.bfloat16)
     items = experts_local * capacity
-    outgoing = outgoing.reshape(devices, items, model_width)
-    arrived = lax.all_to_all(outgoing, ("req", "exp"), split_axis=0, concat_axis=0, tiled=True)
-    rows = arrived.reshape(devices * items, model_width)
-    gate_part = jnp.dot(rows, expert_in[0], preferred_element_type=jnp.float32)
-    up_part = jnp.dot(rows, expert_in[1], preferred_element_type=jnp.float32)
-    row_expert = jnp.arange(devices * items, dtype=jnp.int32) % items // capacity
-    unit_expert = jnp.arange(width_units, dtype=jnp.int32) // FF
-    own = row_expert[:, None] == unit_expert[None, :]
-    inner = jnp.where(own, jax.nn.silu(gate_part) * up_part, 0.0).astype(jnp.bfloat16)
-    outputs = jnp.dot(inner, expert_down, preferred_element_type=jnp.float32).astype(jnp.bfloat16)
-    returned = lax.all_to_all(
-        outputs.reshape(devices, items, model_width),
-        ("req", "exp"),
-        split_axis=0,
-        concat_axis=0,
-        tiled=True,
-    ).reshape(slots, model_width)
-    first = lax.reduce_precision(mix, 8, 7)
-    second = lax.reduce_precision(mix - first, 8, 7)
-    third = mix - first - second
-    terms = jnp.concatenate([first, second, third], axis=0).astype(jnp.bfloat16)
-    mixed = jnp.dot(terms, returned, preferred_element_type=jnp.float32)
-    mixed = mixed.reshape(3, tok_local, model_width)
-    expert_out = (mixed[0] + mixed[1] + mixed[2]).astype(jnp.bfloat16)
+    cut = items * 3 // 5 // 8 * 8
+    bounds = [(0, cut), (cut, items)] if cut else [(0, items)]
+
+    def keys_of(lower, upper):
+        count = upper - lower
+        index = jnp.arange(devices * count, dtype=jnp.int32)
+        slot_ids = index // count * items + lower + index % count
+        return slot_ids // (copies * capacity) * capacity + slot_ids % capacity
+
+    def exchange(block, count):
+        return lax.all_to_all(
+            block.reshape(devices, count, model_width),
+            ("req", "exp"),
+            split_axis=0,
+            concat_axis=0,
+            tiled=True,
+        ).reshape(devices * count, model_width)
+
+    arrived = []
+    for lower, upper in bounds:
+        slot_keys = keys_of(lower, upper)
+        fill = slot_keys[:, None] == places[0][None, :]
+        for choice in range(1, TOP):
+            fill = fill | (slot_keys[:, None] == places[choice][None, :])
+        outgoing = jnp.dot(
+            fill.astype(jnp.bfloat16), normed, preferred_element_type=jnp.float32
+        ).astype(jnp.bfloat16)
+        arrived.append(exchange(outgoing, upper - lower))
+    returned = []
+    for (lower, upper), rows in zip(bounds, arrived):
+        count = upper - lower
+        begin = lower // capacity * FF
+        end = min(width_units, ((upper - 1) // capacity + 1) * FF)
+        gate_part = jnp.dot(rows, expert_in[0, :, begin:end], preferred_element_type=jnp.float32)
+        up_part = jnp.dot(rows, expert_in[1, :, begin:end], preferred_element_type=jnp.float32)
+        inner = jax.nn.silu(gate_part) * up_part
+        if end - begin > FF:
+            row_ids = jnp.arange(devices * count, dtype=jnp.int32)
+            row_expert = (row_ids % count + lower) // capacity
+            unit_expert = jnp.arange(begin, end, dtype=jnp.int32) // FF
+            inner = jnp.where(row_expert[:, None] == unit_expert[None, :], inner, 0.0)
+        outputs = jnp.dot(
+            inner.astype(jnp.bfloat16), expert_down[begin:end], preferred_element_type=jnp.float32
+        ).astype(jnp.bfloat16)
+        returned.append(exchange(outputs, count))
+    total = jnp.zeros((tok_local, model_width), jnp.float32)
+    for (lower, upper), rows in zip(bounds, returned):
+        slot_keys = keys_of(lower, upper)
+        mix = jnp.zeros((tok_local, slot_keys.shape[0]), jnp.float32)
+        for choice in range(TOP):
+            mix = mix + jnp.where(
+                positions[:, choice][:, None] == slot_keys[None, :],
+                gate_weights[:, choice][:, None],
+                0.0,
+            )
+        first = lax.reduce_precision(mix, 8, 7)
+        second = lax.reduce_precision(mix - first, 8, 7)
+        third = mix - first - second
+        terms = jnp.concatenate([first, second, third], axis=0).astype(jnp.bfloat16)
+        mixed = jnp.dot(terms, rows, preferred_element_type=jnp.float32)
+        mixed = mixed.reshape(3, tok_local, model_width)
+        total = total + (mixed[0] + mixed[1] + mixed[2])
+    expert_out = total.astype(jnp.bfloat16)
     return (attended, expert_out)
 
 

time: 462 us -> 430 us (0.931)
  waiting for transfers between devices: 284 us -> 234 us
  starting transfers between devices: 15 us -> 20.9 us
  matrix products: 102 us -> 107 us
    all_to_all x2 -> x4, waiting for transfers between devices: 234 us -> 185 us  [exchange(): lax.all_to_all(block.reshape(devices, count, model_width), ('req', 'exp')...]
    all_to_all x2 -> x4, starting transfers between devices: 7.66 us -> 13.5 us  [exchange(): lax.all_to_all(block.reshape(devices, count, model_width), ('req', 'exp')...]
    dot_general x3 -> x6, matrix products: 54.4 us -> 58.6 us  [the longest x2 34.3 us: local(): jnp.dot(inner.astype(jnp.bfloat16), expert_down[begin:end], preferred_ele...]
  transfers between devices with their start and end apart: 4 -> 6, of which waited for: 4 -> 6; matrix products, arithmetic and copies ran while one was open for 18% -> 33% of each run, Pallas kernels for 0% -> 0%
where the time goes in v2:
time: 430 us; the launch traced here: 429 us
  waiting for transfers between devices  234 us (54%)
  matrix products  107 us (25%)
  local copies, waits for them, and re-layouts  30.9 us (7%)
  other arithmetic  21.2 us (5%)
  starting transfers between devices  20.9 us (5%)
  between operations  14.2 us (3%)
    all_to_all x4, waiting for transfers between devices, exchange(): lax.all_to_all(block.reshape(devices, count, model_width), ('req', 'exp')...  185 us
    dot_general x2, matrix products, local(): jnp.dot(inner.astype(jnp.bfloat16), expert_down[begin:end], preferred_ele...  34.3 us
    all_to_all x1, waiting for transfers between devices, local(): lax.all_to_all(attention, 'exp', split_axis=0, concat_axis=1, tiled=True)  29 us
    all_gather x1, waiting for transfers between devices, local(): full_proj = lax.all_gather(out_proj, 'exp', axis=0, tiled=True)  19.1 us
    dot_general x2, matrix products, attend_request(): jnp.einsum('thd,jhd->htj', query_heads, cache_keys, preferred_element_typ...  18.8 us
    dot_general x2, matrix products, local(): jnp.dot(rows, expert_in[0, :, begin:end], preferred_element_type=jnp.floa...  18.3 us
    dot_general x2, matrix products, attend_request(): jnp.einsum('htj,jhd->thd', weights_bf, all_vals, preferred_element_type=j...  17.9 us
    reduce_sum x2, other arithmetic, attend_request(): denoms = jnp.sum(weights, axis=-1)  16.5 us
  transfers between devices with their start and end apart: 6, of which 6 were waited for; matrix products, arithmetic and copies ran while one was open for 33% of the time, Pallas kernels for 0%

profile of v2, /device:TPU:0, one launch (start us, length us, event | category | flops | bytes accessed | tf_op | source)
XLA Modules:
  0.0 429.0 jit_solution(5335039157397599980)
XLA Ops:
  7.9 82.7 %while.10 = (s32[]{:T(128)}, bf16[2,512,256]{2,1,0:T(8,128)(2,1)}, bf16[2,2,4096,256]{3,2,1,0:T(8,128)(2,1)}, bf16[2,2,512,256]{3,2,1,0:T(8,128)(2,1)}, s32[2]{0...) while((s32[]{:T(128)}, bf16[2,512,256]{2,1,0:T(8,128)(2,1)}, ...), condition=%wide.region_4.5_spmd, body=%wide.region_0.4_spmd.sunk | while | flops 2463631360 | bytes 102543704 | solution.py:70
  7.9 3.8 constant_dynamic-slice_fusion.10
  11.8 4.1 copy.62
  17.5 9.1 %fusion.186 = (f32[2,512]{1,0:T(2,128)S(1)}, f32[2,512,4096]{2,1,0:T(8,128)}) fusion(bf16[512,2,128]{0,2,1:T(8,128)(2,1)S(1)} %bitcast.135, bf16[4096,2,128]{0,2,1:T(8,128)(2,1)} %bitcast.134, pred[4096]{0:T(1024)(128)(4,1)S(1)} %iota_compare_fusion.8), kind=kOutput, calls=%fused_computation.214.clone.1 | convolution fusion | flops 1086323712 | bytes 19144704 | tf_op jit(solution)/shard_map/while/body/eval_jaxpr/thd,jhd->htj/dot_general | solution.py:42
  27.6 8.3 %fusion.187 = f32[2,512]{1,0:T(2,128)S(1)} fusion(f32[2,512,512]{2,1,0:T(8,128)S(1)} %get-tuple-element.152, f32[2,512,4096]{2,1,0:T(8,128)} %get-tuple-element.154, f32[2,512]{1,0:T(2,128)S(1)} %reduce_max.27), kind=kLoop, calls=%fused_computation.3.clone.1 | loop fusion | flops 14154752 | bytes 18882560 | tf_op jit(solution)/shard_map/while/body/eval_jaxpr/reduce_sum | solution.py:63
  39.1 9.0 %fusion.188 = bf16[512,2,128]{0,2,1:T(8,128)(2,1)S(1)} fusion(f32[2,512,512]{2,1,0:T(8,128)} %copy-done, f32[2,512,4096]{2,1,0:T(8,128)} %get-tuple-element.154, f32[2,512]{1,0:T(2,128)S(1)} %reduce_max.27, bf16[512,2,128]{0,2,1:T(8,128)(2,1)S(1)} %bitcast.140, bf16[4096,2,128]{0,2,1:T(8,128)(2,1)} %bitcast.137, f32[512,2]{0,1:T(2,128)S(1)} %bitcast.151), kind=kOutput, calls=%fused_computation.13.clone.1 | convolution fusion | flops 1227096064 | bytes 21504000 | tf_op jit(solution)/shard_map/while/body/eval_jaxpr/htj,jhd->thd/dot_general | solution.py:66
  49.1 3.8 constant_dynamic-slice_fusion.10
  52.9 4.1 copy.62
  58.6 9.7 %fusion.186 = (f32[2,512]{1,0:T(2,128)S(1)}, f32[2,512,4096]{2,1,0:T(8,128)}) fusion(bf16[512,2,128]{0,2,1:T(8,128)(2,1)S(1)} %bitcast.135, bf16[4096,2,128]{0,2,1:T(8,128)(2,1)} %bitcast.134, pred[4096]{0:T(1024)(128)(4,1)S(1)} %iota_compare_fusion.8), kind=kOutput, calls=%fused_computation.214.clone.1 | convolution fusion | flops 1086323712 | bytes 19144704 | tf_op jit(solution)/shard_map/while/body/eval_jaxpr/thd,jhd->htj/dot_general | solution.py:42
  69.3 8.3 %fusion.187 = f32[2,512]{1,0:T(2,128)S(1)} fusion(f32[2,512,512]{2,1,0:T(8,128)S(1)} %get-tuple-element.152, f32[2,512,4096]{2,1,0:T(8,128)} %get-tuple-element.154, f32[2,512]{1,0:T(2,128)S(1)} %reduce_max.27), kind=kLoop, calls=%fused_computation.3.clone.1 | loop fusion | flops 14154752 | bytes 18882560 | tf_op jit(solution)/shard_map/while/body/eval_jaxpr/reduce_sum | solution.py:63
  80.8 8.9 %fusion.188 = bf16[512,2,128]{0,2,1:T(8,128)(2,1)S(1)} fusion(f32[2,512,512]{2,1,0:T(8,128)} %copy-done, f32[2,512,4096]{2,1,0:T(8,128)} %get-tuple-element.154, f32[2,512]{1,0:T(2,128)S(1)} %reduce_max.27, bf16[512,2,128]{0,2,1:T(8,128)(2,1)S(1)} %bitcast.140, bf16[4096,2,128]{0,2,1:T(8,128)(2,1)} %bitcast.137, f32[512,2]{0,1:T(2,128)S(1)} %bitcast.151), kind=kOutput, calls=%fused_computation.13.clone.1 | convolution fusion | flops 1227096064 | bytes 21504000 | tf_op jit(solution)/shard_map/while/body/eval_jaxpr/htj,jhd->thd/dot_general | solution.py:66
  90.6 7.3 %all-to-all-start = ((bf16[8,128,256]{2,1,0:T(8,128)(2,1)}), bf16[8,128,256]{2,1,0:T(8,128)(2,1)S(1)}, u32[]{:S(2)}, u32[]{:S(2)}) async-start(bf16[8,128,256]{2,1,0:T(8,128)(2,1)} %bitcast.150), calls=%async_computation | async-start | bytes 1048576 | tf_op jit(solution)/shard_map/all_to_all | solution.py:72
  98.2 29.0 %all-to-all-done = bf16[8,128,256]{2,1,0:T(8,128)(2,1)S(1)} async-done(((bf16[8,128,256]{2,1,0:T(8,128)(2,1)}), bf16[8,128,256]{2,1,0:T(8,128)(2,1)S(1)}, u32[]{:S(2)}, u32[]{:S(2)}) %all-to-all-start) | async-done | bytes 524320 | tf_op jit(solution)/shard_map/all_to_all | solution.py:72
  127.5 19.1 %all-gather.2.cloned.1.call-done = bf16[2048,2048]{1,0:T(8,128)(2,1)} async-done(((bf16[256,2048]{1,0:T(8,128)(2,1)}), bf16[2048,2048]{1,0:T(8,128)(2,1)}) %all-gather.2.cloned.1.call-update) | async-done | bytes 8388624 | tf_op jit(solution)/shard_map/all_gather | solution.py:31
  146.6 5.5 %multiply_reduce_fusion = (f32[128]{0:T(128)S(1)}, bf16[128,2048]{1,0:T(8,128)(2,1)}, f32[128,2048]{1,0:T(8,128)S(1)}) fusion(bf16[128,2048]{0,1:T(8,128)(2,1)S(1)} %bitcast.142, bf16[2048,2048]{1,0:T(8,128)(2,1)} %all-gather.2.cloned.1.call-done, bf16[128,2048]{1,0:T(8,128)(2,1)} %param.18), kind=kOutput, calls=%fused_computation.52 | convolution fusion | flops 1075052416 | bytes 11010560 | tf_op jit(solution)/shard_map/dot_general | solution.py:73
  160.9 47.2 %all-to-all-done.3 = bf16[32,16,2048]{2,1,0:T(8,128)(2,1)S(1)} async-done(((bf16[32,16,2048]{2,1,0:T(8,128)(2,1)}), bf16[32,16,2048]{2,1,0:T(8,128)(2,1)S(1)}, u32[]{:S(2)}, u32[]{:S(2)}) %all-to-all-start.3) | async-done | bytes 2097184 | tf_op jit(solution)/shard_map/all_to_all | solution.py:102
  212.9 6.5 %fusion.33 = f32[512,1024]{1,0:T(8,128)} fusion(bf16[512,2048]{1,0:T(8,128)(2,1)} %bitcast.146, bf16[2,2048,2048]{2,1,0:T(8,128)(2,1)} %param.22), kind=kOutput, calls=%fused_computation.32 | convolution fusion | flops 2147483648 | bytes 8388608 | tf_op jit(solution)/shard_map/dot_general | solution.py:125
  219.4 10.6 %fusion.41 = bf16[512,2048]{1,0:T(8,128)(2,1)} fusion(bf16[2048,2048]{1,0:T(8,128)(2,1)} %param.23, f32[512,1024]{1,0:T(8,128)} %fusion.33, bf16[512,2048]{1,0:T(8,128)(2,1)} %bitcast.147, bf16[2,2048,2048]{2,1,0:T(8,128)(2,1)} %param.22), kind=kOutput, calls=%fused_computation.40 | convolution fusion | flops 4299161600 | bytes 14680064 | tf_op jit(solution)/shard_map/dot_general | solution.py:133
  230.0 55.4 %all-to-all-done.1 = bf16[32,24,2048]{2,1,0:T(8,128)(2,1)S(1)} async-done(((bf16[32,24,2048]{2,1,0:T(8,128)(2,1)}), bf16[32,24,2048]{2,1,0:T(8,128)(2,1)S(1)}, u32[]{:S(2)}, u32[]{:S(2)}) %all-to-all-start.1) | async-done | bytes 3145760 | tf_op jit(solution)/shard_map/all_to_all | solution.py:102
  289.8 11.8 %fusion.27 = f32[768,2048]{1,0:T(8,128)} fusion(bf16[768,2048]{1,0:T(8,128)(2,1)} %bitcast.144, bf16[2,2048,2048]{2,1,0:T(8,128)(2,1)} %param.22), kind=kOutput, calls=%fused_computation.25 | convolution fusion | flops 6442450944 | bytes 17825792 | tf_op jit(solution)/shard_map/dot_general | solution.py:125
  301.5 23.7 %convolution_convert_fusion = bf16[768,2048]{1,0:T(8,128)(2,1)} fusion(bf16[2048,2048]{1,0:T(8,128)(2,1)} %param.23, f32[768,2048]{1,0:T(8,128)} %fusion.27, bf16[768,2048]{1,0:T(8,128)(2,1)} %bitcast.145, bf16[2,2048,2048]{2,1,0:T(8,128)(2,1)} %param.22, s32[2048]{0:T(1024)S(1)} %add_select_fusion, s32[768]{0:T(1024)S(1)} %add_select_fusion.1), kind=kOutput, calls=%fused_computation.38 | convolution fusion | flops 12899057664 | bytes 29371392 | tf_op jit(solution)/shard_map/dot_general | solution.py:133
  325.3 14.6 %all-to-all-done.4 = bf16[32,16,2048]{2,1,0:T(8,128)(2,1)S(1)} async-done(((bf16[32,16,2048]{2,1,0:T(8,128)(2,1)}), bf16[32,16,2048]{2,1,0:T(8,128)(2,1)S(1)}, u32[]{:S(2)}, u32[]{:S(2)}) %all-to-all-start.4) | async-done | bytes 2097184 | tf_op jit(solution)/shard_map/all_to_all | solution.py:102
  341.2 3.8 all-to-all-start.2
  349.2 68.2 %all-to-all-done.2 = bf16[32,24,2048]{2,1,0:T(8,128)(2,1)} async-done(((bf16[32,24,2048]{2,1,0:T(8,128)(2,1)}), bf16[32,24,2048]{2,1,0:T(8,128)(2,1)}, u32[]{:S(2)}, u32[]{:S(2)}) %all-to-all-start.2) | async-done | bytes 3145760 | tf_op jit(solution)/shard_map/all_to_all | solution.py:102
  (88 shorter events, 42.7 us)
Async XLA Ops:
  7.2 139.5 %all-gather.2.cloned.1.call-start = ((), (), s32[]{:S(2)}) async-start(), calls=%async_computation.5 | async-start | bytes 9437184 | tf_op jit(solution)/shard_map/all_gather | solution.py:31
  7.9 90.1 %copy-start.8 = (s32[128,8]{0,1:T(8,128)S(1)}, s32[128,8]{0,1:T(8,128)}, u32[]{:S(2)}) copy-start(s32[128,8]{0,1:T(8,128)} %param.20) | copy-start | bytes 12292
  11.8 4.1 copy-start.3
  11.8 4.3 %copy-start.11 = (s32[2]{0:T(128)S(1)}, s32[2]{0:T(128)}, u32[]{:S(2)}) copy-start(s32[2]{0:T(128)} %get-tuple-element.181) | copy-start | bytes 28 | tf_op jit(solution)/shard_map/while
  17.5 9.2 %copy-start.2 = (bf16[2,2,512,256]{3,2,1,0:T(8,128)(2,1)S(1)}, bf16[2,2,512,256]{3,2,1,0:T(8,128)(2,1)}, u32[]{:S(2)}) copy-start(bf16[2,2,512,256]{3,2,1,0:T(8,128)(2,1)} %get-tuple-element.180) | copy-start | bytes 3145732 | tf_op jit(solution)/shard_map/while
  27.6 8.3 %copy-start = (f32[2,512,512]{2,1,0:T(8,128)}, f32[2,512,512]{2,1,0:T(8,128)S(1)}, u32[]{:S(2)}) copy-start(f32[2,512,512]{2,1,0:T(8,128)S(1)} %get-tuple-element.152) | copy-start | bytes 6291460 | tf_op jit(solution)/shard_map/while
  39.1 9.1 %copy-start.6 = (bf16[2,512,256]{2,1,0:T(8,128)(2,1)S(1)}, bf16[2,512,256]{2,1,0:T(8,128)(2,1)}, u32[]{:S(2)}) copy-start(bf16[2,512,256]{2,1,0:T(8,128)(2,1)} %get-tuple-element.169) | copy-start | bytes 1572868 | tf_op jit(solution)/shard_map/while
  48.3 0.8 copy-start.7
  52.9 4.1 copy-start.3
  52.9 4.3 %copy-start.11 = (s32[2]{0:T(128)S(1)}, s32[2]{0:T(128)}, u32[]{:S(2)}) copy-start(s32[2]{0:T(128)} %get-tuple-element.181) | copy-start | bytes 28 | tf_op jit(solution)/shard_map/while
  58.6 9.7 %copy-start.2 = (bf16[2,2,512,256]{3,2,1,0:T(8,128)(2,1)S(1)}, bf16[2,2,512,256]{3,2,1,0:T(8,128)(2,1)}, u32[]{:S(2)}) copy-start(bf16[2,2,512,256]{3,2,1,0:T(8,128)(2,1)} %get-tuple-element.180) | copy-start | bytes 3145732 | tf_op jit(solution)/shard_map/while
  69.3 8.3 %copy-start = (f32[2,512,512]{2,1,0:T(8,128)}, f32[2,512,512]{2,1,0:T(8,128)S(1)}, u32[]{:S(2)}) copy-start(f32[2,512,512]{2,1,0:T(8,128)S(1)} %get-tuple-element.152) | copy-start | bytes 6291460 | tf_op jit(solution)/shard_map/while
  80.7 9.1 %copy-start.6 = (bf16[2,512,256]{2,1,0:T(8,128)(2,1)S(1)}, bf16[2,512,256]{2,1,0:T(8,128)(2,1)}, u32[]{:S(2)}) copy-start(bf16[2,512,256]{2,1,0:T(8,128)(2,1)} %get-tuple-element.169) | copy-start | bytes 1572868 | tf_op jit(solution)/shard_map/while
  89.8 0.8 copy-start.7
  90.6 36.6 %all-to-all-start = ((bf16[8,128,256]{2,1,0:T(8,128)(2,1)}), bf16[8,128,256]{2,1,0:T(8,128)(2,1)S(1)}, u32[]{:S(2)}, u32[]{:S(2)}) async-start(bf16[8,128,256]{2,1,0:T(8,128)(2,1)} %bitcast.150), calls=%async_computation | async-start | bytes 1048576 | tf_op jit(solution)/shard_map/all_to_all | solution.py:72
  146.6 5.6 %copy-start.9 = (f32[2048]{0:T(1024)S(1)}, f32[2048]{0:T(1024)}, u32[]{:S(2)}) copy-start(f32[2048]{0:T(1024)} %param.19) | copy-start | bytes 24580
  154.4 53.7 %all-to-all-start.3 = ((bf16[32,16,2048]{2,1,0:T(8,128)(2,1)}), bf16[32,16,2048]{2,1,0:T(8,128)(2,1)S(1)}, u32[]{:S(2)}, u32[]{:S(2)}) async-start(bf16[32,16,2048]{2,1,0:T(8,128)(2,1)} %bitcast.43), calls=%async_computation.3 | async-start | bytes 4194304 | tf_op jit(solution)/shard_map/all_to_all | solution.py:102
  208.1 1.4 copy-start.5
  209.5 75.9 %all-to-all-start.1 = ((bf16[32,24,2048]{2,1,0:T(8,128)(2,1)}), bf16[32,24,2048]{2,1,0:T(8,128)(2,1)S(1)}, u32[]{:S(2)}, u32[]{:S(2)}) async-start(bf16[32,24,2048]{2,1,0:T(8,128)(2,1)} %bitcast.37), calls=%async_computation.1 | async-start | bytes 6291456 | tf_op jit(solution)/shard_map/all_to_all | solution.py:102
  285.4 1.7 copy-start.4
  287.0 52.8 %all-to-all-start.4 = ((bf16[32,16,2048]{2,1,0:T(8,128)(2,1)}), bf16[32,16,2048]{2,1,0:T(8,128)(2,1)S(1)}, u32[]{:S(2)}, u32[]{:S(2)}) async-start(bf16[32,16,2048]{2,1,0:T(8,128)(2,1)} %bitcast.148), calls=%async_computation.4 | async-start | bytes 4194304 | tf_op jit(solution)/shard_map/all_to_all | solution.py:102
  339.8 1.4 copy-start.1
  339.8 5.2 %copy-start.10 = (f32[128,8]{0,1:T(8,128)S(1)}, f32[128,8]{0,1:T(8,128)}, u32[]{:S(2)}) copy-start(f32[128,8]{0,1:T(8,128)} %param.21) | copy-start | bytes 12292
  341.2 76.2 %all-to-all-start.2 = ((bf16[32,24,2048]{2,1,0:T(8,128)(2,1)}), bf16[32,24,2048]{2,1,0:T(8,128)(2,1)}, u32[]{:S(2)}, u32[]{:S(2)}) async-start(bf16[32,24,2048]{2,1,0:T(8,128)(2,1)} %bitcast.143), calls=%async_computation.2 | async-start | bytes 6291456 | tf_op jit(solution)/shard_map/all_to_all | solution.py:102
Sparse Core Ops, SparseCore 0:
  10.1 136.4 all-gather.1
